TPU v7x, 256 devices: a whole 4x4x8 slice. The times are simulated.
256 devices in a mesh: clip: 4 (over x), task: 64 (over y, z, core).
Axes of the slice: x: 4, y: 4, z: 8, core: 2. Of those that a mesh axis runs over, the one named last changes fastest.
Arguments:
- latents: bfloat16 [4, 256, 96, 384], P('clip', 'task'), may hold values from -6 to 6
- caches: bfloat16 [4, 64, 3, 2, 96, 384], P('clip', 'task'), may hold values from -6 to 6
- reward_grad: bfloat16 [4, 256, 96, 384], P('clip', 'task'), may hold values from -6 to 6
- weights: bfloat16 [3, 3, 384, 384], replicated, may hold values from -0.1875 to 0.1875
- biases: float32 [3, 384], replicated, may hold values from -3 to 3
- selected: int32 [4, 32], P('clip'), may hold values from 0 to 63, as said below
- destination: int32 [4, 64], P('clip', 'task'), may hold values from 0 to 3
Outputs:
- latent_grad: bfloat16 [4, 256, 96, 384], P('clip', 'task')
- replica_wgrad: float32 [4, 3456, 384], P('clip', 'task')
Inputs may be any that keep to these rules, and one draw needn't show every extreme that they name: The entries of each row of selected are distinct.
All inputs are finite; a program needn't handle non-finite values.
Results may differ from a plain program's by a relative error of at most 0.0065.
Values may be sent and summed in bfloat16 or wider, within the bound.
A program may use at most 128 MiB of HBM per device.

v0:
```python
import jax
import jax.numpy as jnp
from jax import lax
from jax.sharding import PartitionSpec as P


def shifted(block, axis, distance):
    devices = range(lax.axis_size(axis))
    route = [(i - distance, i) for i in devices if i - distance in devices]
    return lax.ppermute(block, axis, route)


def group_forward(cache, latent, weights, biases):
    frames, spots, width = latent.shape
    rows = frames * spots
    layers, taps = (weights.shape[0], weights.shape[1])
    hidden = latent
    extended = []
    preacts = []
    for layer in range(layers):
        joined = jnp.concatenate([cache[layer], hidden], 0)
        total = jnp.zeros((rows, width), jnp.float32) + biases[layer][None, :]
        for tap in range(taps):
            window = joined[tap : tap + frames].reshape(rows, width)
            total = total + jnp.dot(window, weights[layer, tap], preferred_element_type=jnp.float32)
        hidden = (
            hidden.astype(jnp.float32) + jax.nn.silu(total).reshape(frames, spots, width)
        ).astype(jnp.bfloat16)
        extended.append(joined)
        preacts.append(total)
    return (jnp.stack(extended), jnp.stack(preacts))


def layer_backward(preact, kernel, grad, spots):
    rows, width = grad.shape
    taps = kernel.shape[0]
    lead = (taps - 1) * spots
    sigma = jax.nn.sigmoid(preact)
    delta = (grad * sigma * (1.0 + preact * (1.0 - sigma))).astype(jnp.bfloat16)
    ext_grad = jnp.zeros((rows + lead, width), jnp.float32)
    for tap in range(taps):
        part = lax.dot_general(
            delta, kernel[tap], (((1,), (1,)), ((), ())), preferred_element_type=jnp.float32
        )
        ext_grad = ext_grad.at[tap * spots : tap * spots + rows].add(part)
    return (delta, ext_grad)


def add_tail(grad, ext_grad, incoming_layer, lead):
    rows, width = grad.shape
    tail = jnp.concatenate(
        [jnp.zeros((rows - lead, width), jnp.float32), incoming_layer.astype(jnp.float32)], 0
    )
    return grad + ext_grad[lead:] + tail


def kernel_grads(extended, deltas, taps, spots):
    layers = extended.shape[1]
    rows = deltas.shape[2]
    blocks = []
    for layer in range(layers):
        for tap in range(taps):
            window = extended[:, layer, tap * spots : tap * spots + rows]
            blocks.append(
                jnp.einsum(
                    "nrc,nrd->cd", window, deltas[:, layer], preferred_element_type=jnp.float32
                )
            )
    return jnp.concatenate(blocks, 0)


def body(latents, caches, reward_grad, weights, biases, selected, destination):
    latent = latents[0]
    cache = caches[0, 0]
    frames, spots, width = latent.shape
    rows = frames * spots
    layers, taps = (weights.shape[0], weights.shape[1])
    lead = (taps - 1) * spots
    position = lax.axis_index("task")
    clips = lax.axis_size("clip")
    flag = jnp.any(selected[0] == position).astype(jnp.float32)
    extended, preacts = group_forward(cache, latent, weights, biases)
    upstream = reward_grad[0].reshape(rows, width).astype(jnp.float32) * flag
    grad = upstream
    delta_list = [None] * layers
    for layer in range(layers - 1, -1, -1):
        delta, ext_grad = layer_backward(preacts[layer], weights[layer], grad, spots)
        leaving = ext_grad[:lead].astype(jnp.bfloat16)
        arrived = shifted(leaving, "task", -1)
        grad = add_tail(grad, ext_grad, arrived, lead)
        delta_list[layer] = delta
    latent_grad = grad.astype(jnp.bfloat16)
    deltas = jnp.stack(delta_list)
    flat_ext = extended.reshape(layers, (frames + taps - 1) * spots, width)
    replica_ids = jnp.arange(clips, dtype=jnp.int32)
    slot_mask = (replica_ids == destination[0, 0]).astype(jnp.bfloat16)
    send_ext = slot_mask[:, None, None, None] * flat_ext[None]
    send_delta = slot_mask[:, None, None, None] * deltas[None]
    got_ext, got_delta = (
        lax.all_to_all(send_ext, "clip", split_axis=0, concat_axis=0, tiled=True),
        lax.all_to_all(send_delta, "clip", split_axis=0, concat_axis=0, tiled=True),
    )
    local = kernel_grads(got_ext, got_delta, taps, spots)
    block = lax.psum_scatter(local, "task", scatter_dimension=0, tiled=True)
    return (latent_grad.reshape(1, frames, spots, width), block[None])


def solution(mesh):
    in_specs = (
        P("clip", "task", None, None),
        P("clip", "task", None, None, None, None),
        P("clip", "task", None, None),
        P(),
        P(),
        P("clip", None),
        P("clip", "task"),
    )
    out_specs = (P("clip", "task", None, None), P("clip", "task", None))
    return jax.shard_map(body, mesh=mesh, in_specs=in_specs, out_specs=out_specs, check_vma=False)
```

profile of v0, /device:TPU:17, one launch (start us, length us, event | category | flops | bytes accessed | tf_op | source)
XLA Modules:
  0.0 387.4 jit_solution(7618645746623229320)
XLA Ops:
  0.7 1.9 slice_bitcast_fusion.32
  2.6 0.8 slice_reduce_fusion.2
  3.4 1.1 fusion.28
  4.5 1.3 convolution_add_fusion.14
  6.2 1.3 add_convert_fusion.2
  7.6 0.6 compare_reduce_fusion
  12.9 2.6 collective-permute-start
  15.5 4.3 %collective-permute-done = bf16[192,384]{1,0:T(8,128)(2,1)S(1)} collective-permute-done((bf16[192,384]{1,0:T(8,128)(2,1)S(1)}, bf16[192,384]{1,0:T(8,128)(2,1)S(1)}, u32[]{:S(2)}, u32[]{:S(2)}) %collective-permute-start) | collective-permute-done | bytes 147488 | tf_op jit(solution)/shard_map/ppermute | solution.py:10
  21.1 5.4 %collective-permute-start.1 = (bf16[192,384]{1,0:T(8,128)(2,1)S(1)}, bf16[192,384]{1,0:T(8,128)(2,1)S(1)}, u32[]{:S(2)}, u32[]{:S(2)}) collective-permute-start(bf16[192,384]{1,0:T(8,128)(2,1)S(1)} %slice.542), channel_id=1, source_target_pairs={{1,0},{2,1},{3,2},{4,3},{5,4},{6,5},{7,6},{8,7},{9,8},{10,9},{11,1... | collective-permute-start | bytes 442376 | tf_op jit(solution)/shard_map/ppermute | solution.py:10
  27.6 1.3 multiply_convert_fusion
  29.0 2.1 broadcast_multiply_fusion.1
  31.2 4.7 %all-to-all-start.1 = ((bf16[4,3,384,384]{3,2,1,0:T(8,128)(2,1)}), bf16[4,3,384,384]{3,2,1,0:T(8,128)(2,1)}, u32[]{:S(2)}, u32[]{:S(2)}) async-start(bf16[4,3,384,384]{3,2,1,0:T(8,128)(2,1)} %broadcast_multiply_fusion.1), calls=%async_computation.1 | async-start | bytes 7077888 | tf_op jit(solution)/shard_map/all_to_all | solution.py:101
  35.9 1.1 pad_maximum_fusion.3
  37.0 1.1 pad_maximum_fusion.1
  38.3 2.9 broadcast_multiply_fusion
  41.2 30.9 %all-to-all-done.1 = bf16[4,3,384,384]{3,2,1,0:T(8,128)(2,1)} async-done(((bf16[4,3,384,384]{3,2,1,0:T(8,128)(2,1)}), bf16[4,3,384,384]{3,2,1,0:T(8,128)(2,1)}, u32[]{:S(2)}, u32[]{:S(2)}) %all-to-all-start.1) | async-done | bytes 3538976 | tf_op jit(solution)/shard_map/all_to_all | solution.py:101
  72.2 5.1 %all-to-all-start = ((bf16[4,3,576,384]{3,2,1,0:T(8,128)(2,1)}), bf16[4,3,576,384]{3,2,1,0:T(8,128)(2,1)}, u32[]{:S(2)}, u32[]{:S(2)}) async-start(bf16[4,3,576,384]{3,2,1,0:T(8,128)(2,1)} %broadcast_multiply_fusion), calls=%async_computation | async-start | bytes 10616832 | tf_op jit(solution)/shard_map/all_to_all | solution.py:100
  77.7 1.4 fusion.12
  79.0 0.7 slice.541
  79.7 8.6 %collective-permute-start.2 = (bf16[192,384]{1,0:T(8,128)(2,1)}, bf16[192,384]{1,0:T(8,128)(2,1)}, u32[]{:S(2)}, u32[]{:S(2)}) collective-permute-start(bf16[192,384]{1,0:T(8,128)(2,1)} %slice.541), channel_id=1, source_target_pairs={{1,0},{2,1},{3,2},{4,3},{5,4},{6,5},{7,6},{8,7},{9,8},{10,9},{11,1... | collective-permute-start | bytes 442376 | tf_op jit(solution)/shard_map/ppermute | solution.py:10
  88.3 43.2 %all-to-all-done = bf16[4,3,576,384]{3,2,1,0:T(8,128)(2,1)} async-done(((bf16[4,3,576,384]{3,2,1,0:T(8,128)(2,1)}), bf16[4,3,576,384]{3,2,1,0:T(8,128)(2,1)}, u32[]{:S(2)}, u32[]{:S(2)}) %all-to-all-start) | async-done | bytes 5308448 | tf_op jit(solution)/shard_map/all_to_all | solution.py:100
  131.6 3.2 fusion.9
  134.8 3.3 fusion.8
  138.1 3.2 fusion.7
  141.3 3.2 fusion.6
  144.5 3.3 fusion.5
  147.8 3.3 fusion.4
  151.1 3.2 fusion.3
  154.4 3.2 fusion.2
  157.6 3.3 fusion.1
  160.9 140.8 %fusion = f32[64,384]{1,0:T(8,128)} fusion(f32[3456,384]{1,0:T(8,128)} %fusion.1), kind=kCustom, calls=%all-reduce-scatter | all-reduce-scatter fusion | flops 1572865 | bytes 5407744
  301.7 1.9 collective-permute-start.11
  303.6 5.4 %collective-permute-start.10 = (f32[64,384]{1,0:T(8,128)}, f32[64,384]{1,0:T(8,128)}, u32[]{:S(2)}, u32[]{:S(2)}) collective-permute-start(f32[64,384]{1,0:T(8,128)} %fusion), channel_id=1, source_target_pairs={{0,8},{1,9},{2,10},{3,11},{4,12},{5,13},{6,14},{7,15},{8,16},{9,17... | collective-permute-start | bytes 294920
  309.1 9.4 %collective-permute-start.9 = (f32[64,384]{1,0:T(8,128)}, f32[64,384]{1,0:T(8,128)}, u32[]{:S(2)}, u32[]{:S(2)}) collective-permute-start(f32[64,384]{1,0:T(8,128)} %fusion), channel_id=1, source_target_pairs={{0,7},{1,8},{2,9},{3,10},{4,11},{5,12},{6,13},{7,14},{8,15},{9,16}... | collective-permute-start | bytes 294920
  318.5 27.9 %collective-permute-start.8 = (f32[64,384]{1,0:T(8,128)}, f32[64,384]{1,0:T(8,128)}, u32[]{:S(2)}, u32[]{:S(2)}) collective-permute-start(f32[64,384]{1,0:T(8,128)} %fusion), channel_id=1, source_target_pairs={{0,6},{1,7},{2,8},{3,9},{4,10},{5,11},{6,12},{7,13},{8,14},{9,15},... | collective-permute-start | bytes 294920
  346.4 1.5 slice.387
  348.0 1.9 collective-permute-start.12
  351.1 5.1 %collective-permute-done.12 = f32[54,384]{1,0:T(8,128)} collective-permute-done((f32[54,384]{1,0:T(8,128)}, f32[54,384]{1,0:T(8,128)}, u32[]{:S(2)}, u32[]{:S(2)}) %collective-permute-start.12) | collective-permute-done | bytes 82976
  356.2 1.9 collective-permute-start.7
  358.1 3.7 collective-permute-start.6
  361.9 2.2 collective-permute-start.5
  364.1 5.3 %collective-permute-start.4 = (f32[64,384]{1,0:T(8,128)}, f32[64,384]{1,0:T(8,128)S(1)}, u32[]{:S(2)}, u32[]{:S(2)}) collective-permute-start(f32[64,384]{1,0:T(8,128)} %fusion), channel_id=1, source_target_pairs={{0,2},{1,3},{2,4},{3,5},{4,6},{5,7},{6,8},{7,9},{8,10},{9,11},{10,... | collective-permute-start | bytes 294920
  369.3 2.2 collective-permute-start.3
  371.6 2.3 fusion.18
  373.8 1.5 collective-permute-done.5
  376.0 0.6 copy-done.11
  376.6 10.1 %concatenate.56 = f32[694,384]{1,0:T(8,128)S(1)} concatenate(f32[54,384]{1,0:T(8,128)} %collective-permute-done.12, f32[64,384]{1,0:T(8,128)} %collective-permute-done.11, f32[64,384]{1,0:T(8,128)} %collective-permute-done.10, f32[64,384]{1,0:T(8,128)} %collective-permute-done.9, f32[64,384]{1,0:T(8,128)} %collective-permute-done.8, f32[64,384]{1,0:T(8,128)} %copy-done.8, ...), dimensions={0} | concatenate | bytes 2131968
  386.7 0.7 copy.25
  (69 shorter events, 8.0 us)
Async XLA Ops:
  0.6 5.5 %copy-start.2 = (bf16[1,4,96,384]{3,2,1,0:T(8,128)(2,1)S(1)}, bf16[1,4,96,384]{3,2,1,0:T(8,128)(2,1)}, u32[]{:S(2)}) copy-start(bf16[1,4,96,384]{3,2,1,0:T(8,128)(2,1)} %param.25) | copy-start | bytes 884740
  0.6 5.2 %copy-start = (bf16[3,3,384,384]{3,2,1,0:T(8,128)(2,1)S(1)}, bf16[3,3,384,384]{3,2,1,0:T(8,128)(2,1)}, u32[]{:S(2)}) copy-start(bf16[3,3,384,384]{3,2,1,0:T(8,128)(2,1)} %param.28) | copy-start | bytes 7962628
  2.6 4.9 %copy-start.5 = (bf16[2,96,384]{2,1,0:T(8,128)(2,1)}, bf16[2,96,384]{2,1,0:T(8,128)(2,1)S(1)}, u32[]{:S(2)}) copy-start(bf16[2,96,384]{2,1,0:T(8,128)(2,1)S(1)} %get-tuple-element.123) | copy-start | bytes 442372
  2.6 7.7 %copy-start.4 = (bf16[2,96,384]{2,1,0:T(8,128)(2,1)}, bf16[2,96,384]{2,1,0:T(8,128)(2,1)S(1)}, u32[]{:S(2)}) copy-start(bf16[2,96,384]{2,1,0:T(8,128)(2,1)S(1)} %get-tuple-element.122) | copy-start | bytes 442372
  6.2 1.4 copy-start.13
  8.9 1.0 copy-start.15
  9.6 1.0 copy-start.7
  9.8 0.9 copy-start.6
  10.6 1.4 copy-start.3
  12.9 6.9 %collective-permute-start = (bf16[192,384]{1,0:T(8,128)(2,1)S(1)}, bf16[192,384]{1,0:T(8,128)(2,1)S(1)}, u32[]{:S(2)}, u32[]{:S(2)}) collective-permute-start(bf16[192,384]{1,0:T(8,128)(2,1)S(1)} %slice.543), channel_id=1, source_target_pairs={{1,0},{2,1},{3,2},{4,3},{5,4},{6,5},{7,6},{8,7},{9,8},{10,9},{11,1... | collective-permute-start | bytes 442376 | tf_op jit(solution)/shard_map/ppermute | solution.py:10
  20.3 7.3 %copy-start.14 = (f32[384,384]{1,0:T(8,128)S(1)}, f32[384,384]{1,0:T(8,128)}, u32[]{:S(2)}) copy-start(f32[384,384]{1,0:T(8,128)} %get-tuple-element.128) | copy-start | bytes 1769476
  21.1 6.5 %collective-permute-start.1 = (bf16[192,384]{1,0:T(8,128)(2,1)S(1)}, bf16[192,384]{1,0:T(8,128)(2,1)S(1)}, u32[]{:S(2)}, u32[]{:S(2)}) collective-permute-start(bf16[192,384]{1,0:T(8,128)(2,1)S(1)} %slice.542), channel_id=1, source_target_pairs={{1,0},{2,1},{3,2},{4,3},{5,4},{6,5},{7,6},{8,7},{9,8},{10,9},{11,1... | collective-permute-start | bytes 442376 | tf_op jit(solution)/shard_map/ppermute | solution.py:10
  28.9 48.3 %copy-start.1 = (bf16[384,384]{1,0:T(8,128)(2,1)}, bf16[384,384]{1,0:T(8,128)(2,1)S(1)}, u32[]{:S(2)}) copy-start(bf16[384,384]{1,0:T(8,128)(2,1)S(1)} %get-tuple-element.133) | copy-start | bytes 884740
  31.2 41.0 %all-to-all-start.1 = ((bf16[4,3,384,384]{3,2,1,0:T(8,128)(2,1)}), bf16[4,3,384,384]{3,2,1,0:T(8,128)(2,1)}, u32[]{:S(2)}, u32[]{:S(2)}) async-start(bf16[4,3,384,384]{3,2,1,0:T(8,128)(2,1)} %broadcast_multiply_fusion.1), calls=%async_computation.1 | async-start | bytes 7077888 | tf_op jit(solution)/shard_map/all_to_all | solution.py:101
  72.2 59.4 %all-to-all-start = ((bf16[4,3,576,384]{3,2,1,0:T(8,128)(2,1)}), bf16[4,3,576,384]{3,2,1,0:T(8,128)(2,1)}, u32[]{:S(2)}, u32[]{:S(2)}) async-start(bf16[4,3,576,384]{3,2,1,0:T(8,128)(2,1)} %broadcast_multiply_fusion), calls=%async_computation | async-start | bytes 10616832 | tf_op jit(solution)/shard_map/all_to_all | solution.py:100
  79.7 268.2 %collective-permute-start.2 = (bf16[192,384]{1,0:T(8,128)(2,1)}, bf16[192,384]{1,0:T(8,128)(2,1)}, u32[]{:S(2)}, u32[]{:S(2)}) collective-permute-start(bf16[192,384]{1,0:T(8,128)(2,1)} %slice.541), channel_id=1, source_target_pairs={{1,0},{2,1},{3,2},{4,3},{5,4},{6,5},{7,6},{8,7},{9,8},{10,9},{11,1... | collective-permute-start | bytes 442376 | tf_op jit(solution)/shard_map/ppermute | solution.py:10
  160.9 189.0 %copy-start.12 = (u32[256]{0:T(256)S(1)}, u32[256]{0:T(256)}, u32[]{:S(2)}) copy-start(u32[256]{0:T(256)} %constant.235) | copy-start | bytes 3076
  301.7 56.4 %collective-permute-start.11 = (f32[64,384]{1,0:T(8,128)}, f32[64,384]{1,0:T(8,128)}, u32[]{:S(2)}, u32[]{:S(2)}) collective-permute-start(f32[64,384]{1,0:T(8,128)} %fusion), channel_id=1, source_target_pairs={{0,9},{1,10},{2,11},{3,12},{4,13},{5,14},{6,15},{7,16},{8,17},{9,1... | collective-permute-start | bytes 294920
  303.6 58.2 %collective-permute-start.10 = (f32[64,384]{1,0:T(8,128)}, f32[64,384]{1,0:T(8,128)}, u32[]{:S(2)}, u32[]{:S(2)}) collective-permute-start(f32[64,384]{1,0:T(8,128)} %fusion), channel_id=1, source_target_pairs={{0,8},{1,9},{2,10},{3,11},{4,12},{5,13},{6,14},{7,15},{8,16},{9,17... | collective-permute-start | bytes 294920
  309.1 55.0 %collective-permute-start.9 = (f32[64,384]{1,0:T(8,128)}, f32[64,384]{1,0:T(8,128)}, u32[]{:S(2)}, u32[]{:S(2)}) collective-permute-start(f32[64,384]{1,0:T(8,128)} %fusion), channel_id=1, source_target_pairs={{0,7},{1,8},{2,9},{3,10},{4,11},{5,12},{6,13},{7,14},{8,15},{9,16}... | collective-permute-start | bytes 294920
  318.5 50.8 %collective-permute-start.8 = (f32[64,384]{1,0:T(8,128)}, f32[64,384]{1,0:T(8,128)}, u32[]{:S(2)}, u32[]{:S(2)}) collective-permute-start(f32[64,384]{1,0:T(8,128)} %fusion), channel_id=1, source_target_pairs={{0,6},{1,7},{2,8},{3,9},{4,10},{5,11},{6,12},{7,13},{8,14},{9,15},... | collective-permute-start | bytes 294920
  348.0 8.2 %collective-permute-start.12 = (f32[54,384]{1,0:T(8,128)}, f32[54,384]{1,0:T(8,128)}, u32[]{:S(2)}, u32[]{:S(2)}) collective-permute-start(f32[54,384]{1,0:T(8,128)} %slice.387), channel_id=1, source_target_pairs={{0,10},{1,11},{2,12},{3,13},{4,14},{5,15},{6,16},{7,17},{8,18},{9,... | collective-permute-start | bytes 248840
  356.2 17.6 %collective-permute-start.7 = (f32[64,384]{1,0:T(8,128)}, f32[64,384]{1,0:T(8,128)S(1)}, u32[]{:S(2)}, u32[]{:S(2)}) collective-permute-start(f32[64,384]{1,0:T(8,128)} %fusion), channel_id=1, source_target_pairs={{0,5},{1,6},{2,7},{3,8},{4,9},{5,10},{6,11},{7,12},{8,13},{9,14},{... | collective-permute-start | bytes 294920
  358.1 15.7 %collective-permute-start.6 = (f32[64,384]{1,0:T(8,128)}, f32[64,384]{1,0:T(8,128)S(1)}, u32[]{:S(2)}, u32[]{:S(2)}) collective-permute-start(f32[64,384]{1,0:T(8,128)} %fusion), channel_id=1, source_target_pairs={{0,4},{1,5},{2,6},{3,7},{4,8},{5,9},{6,10},{7,11},{8,12},{9,13},{1... | collective-permute-start | bytes 294920
  361.9 13.4 %collective-permute-start.5 = (f32[64,384]{1,0:T(8,128)}, f32[64,384]{1,0:T(8,128)S(1)}, u32[]{:S(2)}, u32[]{:S(2)}) collective-permute-start(f32[64,384]{1,0:T(8,128)} %fusion), channel_id=1, source_target_pairs={{0,3},{1,4},{2,5},{3,6},{4,7},{5,8},{6,9},{7,10},{8,11},{9,12},{10... | collective-permute-start | bytes 294920
  364.1 11.9 %collective-permute-start.4 = (f32[64,384]{1,0:T(8,128)}, f32[64,384]{1,0:T(8,128)S(1)}, u32[]{:S(2)}, u32[]{:S(2)}) collective-permute-start(f32[64,384]{1,0:T(8,128)} %fusion), channel_id=1, source_target_pairs={{0,2},{1,3},{2,4},{3,5},{4,6},{5,7},{6,8},{7,9},{8,10},{9,11},{10,... | collective-permute-start | bytes 294920
  369.3 7.3 %collective-permute-start.3 = (f32[64,384]{1,0:T(8,128)}, f32[64,384]{1,0:T(8,128)}, u32[]{:S(2)}, u32[]{:S(2)}) collective-permute-start(f32[64,384]{1,0:T(8,128)} %fusion), channel_id=1, source_target_pairs={{0,1},{1,2},{2,3},{3,4},{4,5},{5,6},{6,7},{7,8},{8,9},{9,10},{10,1... | collective-permute-start | bytes 294920
  373.8 2.1 copy-start.8
  373.8 2.1 copy-start.9
  375.3 0.6 copy-start.10
  376.0 0.6 copy-start.11
where the time goes:
time: 390 us; the launch traced here: 387 us
  blocking collectives  141 us (36%)
  starting transfers between devices  88.2 us (23%)
  waiting for transfers between devices  86.1 us (22%)
  matrix products  41.7 us (11%)
  local copies, waits for them, and re-layouts  17.9 us (5%)
  other arithmetic  9.57 us (2%)
    unnamed x1, blocking collectives  141 us
    unnamed x10, starting transfers between devices  61.9 us
    all_to_all x1, waiting for transfers between devices, body(): lax.all_to_all(send_ext, 'clip', split_axis=0, concat_axis=0, tiled=True)  43.2 us
    all_to_all x1, waiting for transfers between devices, body(): lax.all_to_all(send_delta, 'clip', split_axis=0, concat_axis=0, tiled=True)  30.9 us
    dot_general x9, matrix products, kernel_grads(): jnp.einsum('nrc,nrd->cd', window, deltas[:, layer], preferred_element_typ...  29.3 us
    ppermute x3, starting transfers between devices, shifted(): return lax.ppermute(block, axis, route)  16.6 us
    unnamed x36, local copies, waits for them, and re-layouts  14.2 us
  transfers between devices with their start and end apart: 15, of which 7 were waited for; matrix products, arithmetic and copies ran while one was open for 47% of the time, Pallas kernels for 0%

commit v1 on v0

v1 whole, which is shorter than its diff:
```python
import jax
import jax.numpy as jnp
from jax import lax
from jax.experimental import pallas as pl
from jax.experimental.pallas import tpu as pltpu
from jax.sharding import PartitionSpec as P

MESH = pl.DeviceIdType.MESH
F32 = jnp.float32
BF16 = jnp.bfloat16

CH = 384
FRAMES = 4
TAPS = 3
LAYERS = 3
SPOTS = 96
ROWS = FRAMES * SPOTS
NX, NY, NZ = 4, 4, 8
KR = TAPS * CH
SL = KR // 8
UNIT = SL // 8
WIDTH_B = (256, 128, 256)


def cols(layer, path):
    wb = WIDTH_B[layer]
    return (wb, CH) if path == 0 else (0, wb)


def width(layer, path):
    lo, hi = cols(layer, path)
    return hi - lo


def task_of(y, z, c):
    return y * 16 + z * 2 + c


def unit_target(layer, unit):
    u = layer * 64 + unit
    return u // 3, u % 3


def kernel(*refs):
    it = iter(refs)
    take = lambda n: [next(it) for _ in range(n)]
    lat_hbm, cache_hbm, rg_hbm, w_hbm, bias_ref, sel_ref, dest_ref = take(7)
    latout_hbm, wg_ref = take(2)
    w_ref, e_ref, rg_ref, sp_ref, g_ref, dpad_ref, leave_ref, in_ref, latg_ref = take(9)
    gbuf = [take(2) for _ in range(LAYERS)]
    r1 = [take(2) for _ in range(LAYERS)]
    s2 = [take(2) for _ in range(LAYERS)]
    r2 = [take(2) for _ in range(LAYERS)]
    s3 = [take(2) for _ in range(LAYERS)]
    r3 = [take(2) for _ in range(LAYERS)]
    fs = [take(2) for _ in range(LAYERS)]
    (tmp_ref, mask_own, mask_ref, fin_ref) = take(4)
    (ld_sem, ch_s, ch_r, mk_s, mk_r, s1_s, s1_r, s2_s, s2_r, s3_s, s3_r, fn_s, fn_r, out_sem) = take(14)

    x = lax.axis_index("clip")
    pos = lax.axis_index("task")
    y = pos // 16
    z = (pos % 16) // 2
    c = pos % 2

    loads = {}
    def load(name, src, dst, k):
        loads[name] = pltpu.make_async_copy(src, dst, ld_sem.at[k])
        loads[name].start()
    load("lat", lat_hbm.at[0], e_ref.at[0, pl.ds(2, 4)], 0)
    for l in range(LAYERS):
        load(("c", l), cache_hbm.at[0, 0, l], e_ref.at[l, pl.ds(0, 2)], 1 + l)
        load(("w", l), w_hbm.at[l], w_ref.at[l], 4 + l)
    load("rg", rg_hbm.at[0], rg_ref, 7)

    def dev(xx, tt):
        return {"clip": xx, "task": tt}

    def b1(o):
        s = (2 * y + c + o) % 8
        return dev(x, task_of(s // 2, z, s % 2))

    def a1(o):
        s = (2 * x + c + o) % 8
        return dev(s // 2, task_of(y, z, s % 2))

    def px(o):
        return dev((x + o) % 4, pos)

    def py(o):
        return dev(x, task_of((y + o) % 4, z, c))

    def pz(o):
        return dev(x, task_of(y, (z + o) % 8, c))

    unit_b = 8 * (2 * y + c) + z
    unit_a = 8 * (2 * x + c) + 2 * y + z % 2

    def final_target(l, path):
        if path == 1:
            t, i = unit_target(l, unit_b)
            return x, t, i
        t, i = unit_target(l, unit_a)
        return z // 2, t, i

    def final_source(i, path):
        u = 3 * pos + i
        j = u % 64
        if path == 1:
            return x, task_of(j // 16, j % 8, (j // 8) % 2)
        return j // 16, task_of((j % 8) // 2, 2 * x + j % 2, (j // 8) % 2)

    barrier = pltpu.get_barrier_semaphore()
    greet = [b1(o) for o in range(1, 8)] + [a1(o) for o in range(1, 8)]
    greet += [px(o) for o in range(1, 4)] + [py(o) for o in range(1, 4)] + [pz(o) for o in range(1, 8)]
    greet += [dev(x, (pos + 1) % 64)]
    greet += [dev(*final_source(i, path)) for i in range(3) for path in range(2)]
    for who in greet:
        pl.semaphore_signal(barrier, inc=1, device_id=who, device_id_type=MESH)

    flag = jnp.max((sel_ref[...] == pos).astype(F32), axis=1, keepdims=True)
    mask = (lax.broadcasted_iota(jnp.int32, (8, 256), 0) == dest_ref[...]).astype(F32)
    mask_own[...] = mask
    mask_ref[1, 2 * y + c] = mask
    mask_ref[0, 2 * x + c] = mask
    dpad_ref[pl.ds(0, 2)] = jnp.zeros((2, SPOTS, CH), BF16)
    dpad_ref[pl.ds(6, 2)] = jnp.zeros((2, SPOTS, CH), BF16)

    @pl.when(pos == 63)
    def _():
        in_ref[...] = jnp.zeros(in_ref.shape, BF16)

    loads["lat"].wait()
    for l in range(LAYERS):
        loads[("c", l)].wait()
        loads[("w", l)].wait()
        lhs = jnp.concatenate([e_ref[l, k:k + 4].reshape(ROWS, CH) for k in range(TAPS)], axis=1)
        a = jnp.dot(lhs, w_ref[l].reshape(KR, CH), preferred_element_type=F32) + bias_ref[l:l + 1, :]
        sg = jax.nn.sigmoid(a)
        sp_ref[l] = sg * (1.0 + a * (1.0 - sg))
        if l < LAYERS - 1:
            h = e_ref[l, 2:6].reshape(ROWS, CH).astype(F32) + a * sg
            e_ref[l + 1, 2:6] = h.astype(BF16).reshape(FRAMES, SPOTS, CH)

    pl.semaphore_wait(barrier, len(greet))
    started = []

    def remote(src, dst, ssem, rsem, who):
        cp = pltpu.make_async_remote_copy(
            src_ref=src, dst_ref=dst, send_sem=ssem, recv_sem=rsem, device_id=who, device_id_type=MESH)
        cp.start()
        started.append(cp)
        return cp

    mk = {}
    for o in range(1, 8):
        mk[1, o] = remote(mask_own, mask_ref.at[1, 2 * y + c], mk_s.at[1, o], mk_r.at[1, o], b1(o))
        mk[0, o] = remote(mask_own, mask_ref.at[0, 2 * x + c], mk_s.at[0, o], mk_r.at[0, o], a1(o))

    loads["rg"].wait()
    g_ref[...] = rg_ref[...].reshape(ROWS, CH).astype(F32) * flag

    mine = [2 * x + c, 2 * y + c]
    first = [a1, b1]
    c1 = {}
    chain = {}
    for l in range(LAYERS - 1, -1, -1):
        if l < LAYERS - 1:
            @pl.when(pos < 63)
            def _(l=l):
                chain[l + 1].wait_recv()
            g_ref[pl.ds(192, 192)] += in_ref[l + 1].astype(F32)
        d = (g_ref[...] * sp_ref[l]).astype(BF16)
        dpad_ref[pl.ds(2, 4)] = d.reshape(FRAMES, SPOTS, CH)
        lhs = jnp.concatenate([dpad_ref[2:4].reshape(192, CH), dpad_ref[1:3].reshape(192, CH)], axis=1)
        rhs = jnp.concatenate([w_ref[l, 0], w_ref[l, 1]], axis=1)
        lead = lax.dot_general(lhs, rhs, (((1,), (1,)), ((), ())), preferred_element_type=F32)
        leave_ref[l] = lead.astype(BF16)
        chain[l] = pltpu.make_async_remote_copy(
            src_ref=leave_ref.at[l], dst_ref=in_ref.at[l], send_sem=ch_s.at[l], recv_sem=ch_r.at[l],
            device_id=dev(x, (pos + 63) % 64), device_id_type=MESH)

        @pl.when(pos > 0)
        def _(l=l):
            chain[l].start()

        pad = jnp.zeros((32, CH), BF16)
        et = jnp.concatenate([v for f in range(6) for v in (e_ref[l, f], pad)], axis=0).T
        et = jnp.concatenate([et[:, 128 * k:128 * k + 512] for k in range(TAPS)], axis=0)
        dp = jnp.concatenate([v for f in range(FRAMES) for v in (dpad_ref[2 + f], pad)], axis=0)
        for path in (1, 0):
            lo, hi = cols(l, path)
            grads = jnp.dot(et, dp[:, lo:hi], preferred_element_type=F32)
            gbuf[l][path][...] = grads.astype(BF16).reshape(8, SL, hi - lo)
            for o in range(1, 8):
                s = (mine[path] + o) % 8
                c1[l, path, o] = remote(
                    gbuf[l][path].at[s], r1[l][path].at[mine[path]],
                    s1_s.at[l, path, o], s1_r.at[l, path, o], first[path](o))
            r1[l][path][mine[path]] = gbuf[l][path][mine[path]]

        lhs = jnp.concatenate([dpad_ref[4 - k:8 - k].reshape(ROWS, CH) for k in range(TAPS)], axis=1)
        rhs = jnp.concatenate([w_ref[l, k] for k in range(TAPS)], axis=1)
        g_ref[...] += lax.dot_general(lhs, rhs, (((1,), (1,)), ((), ())), preferred_element_type=F32)

    @pl.when(pos < 63)
    def _():
        chain[0].wait_recv()
    g_ref[pl.ds(192, 192)] += in_ref[0].astype(F32)
    latg_ref[...] = g_ref[...].astype(BF16).reshape(FRAMES, SPOTS, CH)
    out_copy = pltpu.make_async_copy(latg_ref, latout_hbm.at[0], out_sem)
    out_copy.start()

    for cp in mk.values():
        cp.wait_recv()

    second = [py, px]
    here = [y, x]
    c2, c3 = {}, {}

    def stage1(l, path):
        w = width(l, path)
        for o in range(1, 8):
            c1[l, path, o].wait_recv()

        def step(i, _):
            rows = pl.ds(pl.multiple_of(i * 16, 16), 16)
            raw = [r1[l][path][s, rows, :].astype(F32) for s in range(8)]
            for r in range(4):
                tot = raw[0] * mask_ref[path, 0, r:r + 1, 0:w]
                for s in range(1, 8):
                    tot = tot + raw[s] * mask_ref[path, s, r:r + 1, 0:w]
                if path == 1:
                    s2[l][path][r, rows, :] = tot.astype(BF16)
                else:
                    tmp_ref[r, rows, 0:w] = tot
            return 0

        lax.fori_loop(0, SL // 16, step, 0)
        if path == 0:
            for yy in range(4):
                s2[l][path][yy] = jnp.concatenate(
                    [tmp_ref[r, 36 * yy:36 * yy + 36, 0:w] for r in range(4)], axis=0).astype(BF16)
        for o in range(1, 4):
            c2[l, path, o] = remote(
                s2[l][path].at[(here[path] + o) % 4], r2[l][path].at[here[path]],
                s2_s.at[l, path, o], s2_r.at[l, path, o], second[path](o))
        r2[l][path][here[path]] = s2[l][path][here[path]]

    def stage2(l, path):
        w = width(l, path)
        for o in range(1, 4):
            c2[l, path, o].wait_recv()
        tot = r2[l][path][0].astype(F32)
        for s in range(1, 4):
            tot = tot + r2[l][path][s].astype(F32)
        tot = jnp.concatenate([tot, jnp.zeros((16, w), F32)], axis=0)
        for zz in range(8):
            s3[l][path][zz] = tot[UNIT * zz:UNIT * zz + 32].astype(BF16)
        for o in range(1, 8):
            c3[l, path, o] = remote(
                s3[l][path].at[(z + o) % 8], r3[l][path].at[z],
                s3_s.at[l, path, o], s3_r.at[l, path, o], pz(o))
        r3[l][path][z] = s3[l][path][z]

    finals = []

    def stage3(l, path):
        lo, hi = cols(l, path)
        for o in range(1, 8):
            c3[l, path, o].wait_recv()
        tot = r3[l][path][0].astype(F32)
        for s in range(1, 8):
            tot = tot + r3[l][path][s].astype(F32)
        fs[l][path][...] = tot[0:24]
        xx, tt, i = final_target(l, path)
        own = jnp.logical_and(xx == x, tt == pos)
        dst = fin_ref.at[i, :, lo:hi]
        far = pltpu.make_async_remote_copy(
            src_ref=fs[l][path], dst_ref=dst, send_sem=fn_s.at[l, path], recv_sem=fn_r.at[i],
            device_id=dev(xx, tt), device_id_type=MESH)
        near = pltpu.make_async_copy(fs[l][path], dst, fn_r.at[i])

        @pl.when(own)
        def _():
            near.start()

        @pl.when(jnp.logical_not(own))
        def _():
            far.start()
        finals.append((own, far))

    for l in range(LAYERS - 1, -1, -1):
        for stage in (stage1, stage2, stage3):
            for path in (1, 0):
                stage(l, path)

    for i in range(3):
        pltpu.make_async_copy(fin_ref.at[i], fin_ref.at[i], fn_r.at[i]).wait()
    wg_ref[0] = jnp.concatenate([fin_ref[i, 0:UNIT] for i in range(3)], axis=0)

    for cp in started:
        cp.wait_send()
    for own, far in finals:
        @pl.when(jnp.logical_not(own))
        def _(far=far):
            far.wait_send()

    @pl.when(pos > 0)
    def _():
        for l in range(LAYERS):
            chain[l].wait_send()
    out_copy.wait()


def body(latents, caches, reward_grad, weights, biases, selected, destination):
    vmem = pltpu.VMEM
    per = lambda shape, kind: [vmem(shape(width(l, path)), kind) for l in range(LAYERS) for path in range(2)]
    scratch = [
        vmem((LAYERS, TAPS, CH, CH), BF16),
        vmem((LAYERS, 6, SPOTS, CH), BF16),
        vmem((FRAMES, SPOTS, CH), BF16),
        vmem((LAYERS, ROWS, CH), F32),
        vmem((ROWS, CH), F32),
        vmem((8, SPOTS, CH), BF16),
        vmem((LAYERS, 192, CH), BF16),
        vmem((LAYERS, 192, CH), BF16),
        vmem((FRAMES, SPOTS, CH), BF16),
    ]
    scratch += per(lambda w: (8, SL, w), BF16)
    scratch += per(lambda w: (8, SL, w), BF16)
    scratch += per(lambda w: (4, SL, w), BF16)
    scratch += per(lambda w: (4, SL, w), BF16)
    scratch += per(lambda w: (8, 32, w), BF16)
    scratch += per(lambda w: (8, 32, w), BF16)
    scratch += per(lambda w: (24, w), F32)
    scratch += [
        vmem((4, SL, 256), F32),
        vmem((8, 256), F32),
        vmem((2, 8, 8, 256), F32),
        vmem((3, 24, CH), F32),
    ]
    dma = pltpu.SemaphoreType.DMA
    scratch += [dma((8,)), dma((3,)), dma((3,)), dma((2, 8)), dma((2, 8))]
    scratch += [dma((3, 2, 8)), dma((3, 2, 8)), dma((3, 2, 4)), dma((3, 2, 4)), dma((3, 2, 8)), dma((3, 2, 8))]
    scratch += [dma((3, 2)), dma((3,)), dma(())]
    hbm = pl.BlockSpec(memory_space=pl.ANY)
    near = pl.BlockSpec(memory_space=pltpu.VMEM)
    return pl.pallas_call(
        kernel,
        out_shape=(
            jax.ShapeDtypeStruct((1, FRAMES, SPOTS, CH), BF16),
            jax.ShapeDtypeStruct((1, 3 * UNIT, CH), F32),
        ),
        in_specs=[hbm, hbm, hbm, hbm, near, near, near],
        out_specs=(hbm, near),
        scratch_shapes=scratch,
        compiler_params=pltpu.CompilerParams(
            collective_id=0, has_side_effects=True, vmem_limit_bytes=48 * 1024 * 1024),
        cost_estimate=pl.CostEstimate(flops=3_060_000_000, bytes_accessed=5_000_000, transcendentals=450_000),
    )(latents, caches, reward_grad, weights, biases, selected, destination)


def solution(mesh):
    in_specs = (
        P("clip", "task", None, None),
        P("clip", "task", None, None, None, None),
        P("clip", "task", None, None),
        P(),
        P(),
        P("clip", None),
        P("clip", "task"),
    )
    out_specs = (P("clip", "task", None, None), P("clip", "task", None))
    return jax.shard_map(body, mesh=mesh, in_specs=in_specs, out_specs=out_specs, check_vma=False)
```

time: 390 us -> 82.3 us (0.21)
  the two profiles are of different devices: /device:TPU:17 before, /device:TPU:5 now
where the time goes in v1:
time: 82.3 us; the launch traced here: 82 us
  Pallas kernels  73.2 us (89%)
  local copies, waits for them, and re-layouts  7.46 us (9%)
  between operations  1.3 us (2%)
    pallas_call x1, Pallas kernels, body(): pl.pallas_call(kernel, out_shape=(jax.ShapeDtypeStruct((1, FRAMES, SPOTS,...  73.2 us
    unnamed x13, local copies, waits for them, and re-layouts  6.74 us

profile of v1, /device:TPU:5, one launch (start us, length us, event | category | flops | bytes accessed | tf_op | source)
XLA Modules:
  0.0 82.0 jit_solution(18070972143265068635)
XLA Ops:
  1.3 0.0 copy-start
  1.3 1.7 %copy-done = bf16[3,3,384,384]{3,2,1,0:T(8,128)(2,1)S(1)} copy-done((bf16[3,3,384,384]{3,2,1,0:T(8,128)(2,1)S(1)}, bf16[3,3,384,384]{3,2,1,0:T(8,128)(2,1)}, u32[]{:S(2)}) %copy-start) | copy-done | bytes 2654232
  3.0 0.0 copy-start.1
  3.0 1.0 %copy-done.1 = bf16[1,1,3,2,96,384]{5,4,3,2,1,0:T(8,128)(2,1)S(1)} copy-done((bf16[1,1,3,2,96,384]{5,4,3,2,1,0:T(8,128)(2,1)S(1)}, bf16[1,1,3,2,96,384]{5,4,3,2,1,0:T(8,128)(2,1)}, u32[]{:S(2)}) %copy-start.1) | copy-done | bytes 442392
  4.0 0.0 copy-start.2
  4.0 1.0 %copy-done.2 = bf16[1,4,96,384]{3,2,1,0:T(8,128)(2,1)S(1)} copy-done((bf16[1,4,96,384]{3,2,1,0:T(8,128)(2,1)S(1)}, bf16[1,4,96,384]{3,2,1,0:T(8,128)(2,1)}, u32[]{:S(2)}) %copy-start.2) | copy-done | bytes 294936
  5.0 0.0 copy-start.3
  5.0 1.0 %copy-done.3 = bf16[1,4,96,384]{3,2,1,0:T(8,128)(2,1)S(1)} copy-done((bf16[1,4,96,384]{3,2,1,0:T(8,128)(2,1)S(1)}, bf16[1,4,96,384]{3,2,1,0:T(8,128)(2,1)}, u32[]{:S(2)}) %copy-start.3) | copy-done | bytes 294936
  6.0 0.0 copy-start.4
  6.0 0.7 copy-done.4
  6.7 0.0 copy-start.5
  6.7 0.7 copy-done.5
  7.3 73.2 %shard_map.86 = (bf16[1,4,96,384]{3,2,1,0:T(8,128)(2,1)S(1)}, f32[1,54,384]{2,1,0:T(8,128)S(1)}) custom-call(bf16[1,4,96,384]{3,2,1,0:T(8,128)(2,1)S(1)} %copy-done.2, bf16[1,1,3,2,96,384]{5,4,3,2,1,0:T(8,128)(2,1)S(1)} %copy-done.1, bf16[1,4,96,384]{3,2,1,0:T(8,128)(2,1)S(1)} %copy-done.3, bf16[3,3,384,384]{3,2,1,0:T(8,128)(2,1)S(1)} %copy-done, ...), custom_call_target="tpu_custom_call" | custom-call | flops 3060000000 | bytes 5000000 | tf_op jit(solution)/shard_map/pallas_call | solution.py:349
  80.6 0.7 copy.9
  81.3 0.7 copy.12
Async XLA Ops:
  1.3 1.8 %copy-start = (bf16[3,3,384,384]{3,2,1,0:T(8,128)(2,1)S(1)}, bf16[3,3,384,384]{3,2,1,0:T(8,128)(2,1)}, u32[]{:S(2)}) copy-start(bf16[3,3,384,384]{3,2,1,0:T(8,128)(2,1)} %refs_3_.1) | copy-start | bytes 7962628
  3.0 1.0 %copy-start.1 = (bf16[1,1,3,2,96,384]{5,4,3,2,1,0:T(8,128)(2,1)S(1)}, bf16[1,1,3,2,96,384]{5,4,3,2,1,0:T(8,128)(2,1)}, u32[]{:S(2)}) copy-start(bf16[1,1,3,2,96,384]{5,4,3,2,1,0:T(8,128)(2,1)} %refs_1_.1) | copy-start | bytes 1327108
  4.0 1.0 %copy-start.2 = (bf16[1,4,96,384]{3,2,1,0:T(8,128)(2,1)S(1)}, bf16[1,4,96,384]{3,2,1,0:T(8,128)(2,1)}, u32[]{:S(2)}) copy-start(bf16[1,4,96,384]{3,2,1,0:T(8,128)(2,1)} %refs_0_.1) | copy-start | bytes 884740
  5.0 1.0 %copy-start.3 = (bf16[1,4,96,384]{3,2,1,0:T(8,128)(2,1)S(1)}, bf16[1,4,96,384]{3,2,1,0:T(8,128)(2,1)}, u32[]{:S(2)}) copy-start(bf16[1,4,96,384]{3,2,1,0:T(8,128)(2,1)} %refs_2_.1) | copy-start | bytes 884740
  6.0 0.7 copy-start.4
  6.7 0.7 copy-start.5

commit v2 on v1

--- a/solution.py
+++ b/solution.py
@@ -19,6 +19,7 @@
 KR = TAPS * CH
 SL = KR // 8
 UNIT = SL // 8
+TOP = LAYERS - 1
 WIDTH_B = (256, 128, 256)
 
 
@@ -51,11 +52,11 @@
     r1 = [take(2) for _ in range(LAYERS)]
     s2 = [take(2) for _ in range(LAYERS)]
     r2 = [take(2) for _ in range(LAYERS)]
-    s3 = [take(2) for _ in range(LAYERS)]
-    r3 = [take(2) for _ in range(LAYERS)]
-    fs = [take(2) for _ in range(LAYERS)]
-    (tmp_ref, mask_own, mask_ref, fin_ref) = take(4)
-    (ld_sem, ch_s, ch_r, mk_s, mk_r, s1_s, s1_r, s2_s, s2_r, s3_s, s3_r, fn_s, fn_r, out_sem) = take(14)
+    s3 = take(LAYERS)
+    r3 = take(LAYERS)
+    fs = take(LAYERS)
+    (tmp_ref, mask_ref, fin_ref) = take(3)
+    (ld_sem, ch_s, ch_r, s1_s, s1_r, s2_s, s2_r, s3_s, s3_r, fn_s, fn_r, out_sem) = take(12)
 
     x = lax.axis_index("clip")
     pos = lax.axis_index("task")
@@ -119,10 +120,11 @@
         pl.semaphore_signal(barrier, inc=1, device_id=who, device_id_type=MESH)
 
     flag = jnp.max((sel_ref[...] == pos).astype(F32), axis=1, keepdims=True)
-    mask = (lax.broadcasted_iota(jnp.int32, (8, 256), 0) == dest_ref[...]).astype(F32)
-    mask_own[...] = mask
-    mask_ref[1, 2 * y + c] = mask
-    mask_ref[0, 2 * x + c] = mask
+    for path in range(2):
+        w = width(TOP, path)
+        mask = (lax.broadcasted_iota(jnp.int32, (16, w), 0) == dest_ref[...]).astype(F32).astype(BF16)
+        for s in range(8):
+            gbuf[TOP][path][s, SL:SL + 16] = mask
     dpad_ref[pl.ds(0, 2)] = jnp.zeros((2, SPOTS, CH), BF16)
     dpad_ref[pl.ds(6, 2)] = jnp.zeros((2, SPOTS, CH), BF16)
 
@@ -151,11 +153,6 @@
         cp.start()
         started.append(cp)
         return cp
-
-    mk = {}
-    for o in range(1, 8):
-        mk[1, o] = remote(mask_own, mask_ref.at[1, 2 * y + c], mk_s.at[1, o], mk_r.at[1, o], b1(o))
-        mk[0, o] = remote(mask_own, mask_ref.at[0, 2 * x + c], mk_s.at[0, o], mk_r.at[0, o], a1(o))
 
     loads["rg"].wait()
     g_ref[...] = rg_ref[...].reshape(ROWS, CH).astype(F32) * flag
@@ -191,7 +188,7 @@
         for path in (1, 0):
             lo, hi = cols(l, path)
             grads = jnp.dot(et, dp[:, lo:hi], preferred_element_type=F32)
-            gbuf[l][path][...] = grads.astype(BF16).reshape(8, SL, hi - lo)
+            gbuf[l][path][:, 0:SL] = grads.astype(BF16).reshape(8, SL, hi - lo)
             for o in range(1, 8):
                 s = (mine[path] + o) % 8
                 c1[l, path, o] = remote(
@@ -203,16 +200,15 @@
         rhs = jnp.concatenate([w_ref[l, k] for k in range(TAPS)], axis=1)
         g_ref[...] += lax.dot_general(lhs, rhs, (((1,), (1,)), ((), ())), preferred_element_type=F32)
 
-    @pl.when(pos < 63)
-    def _():
-        chain[0].wait_recv()
-    g_ref[pl.ds(192, 192)] += in_ref[0].astype(F32)
-    latg_ref[...] = g_ref[...].astype(BF16).reshape(FRAMES, SPOTS, CH)
     out_copy = pltpu.make_async_copy(latg_ref, latout_hbm.at[0], out_sem)
-    out_copy.start()
-
-    for cp in mk.values():
-        cp.wait_recv()
+
+    def latent_out():
+        @pl.when(pos < 63)
+        def _():
+            chain[0].wait_recv()
+        g_ref[pl.ds(192, 192)] += in_ref[0].astype(F32)
+        latg_ref[...] = g_ref[...].astype(BF16).reshape(FRAMES, SPOTS, CH)
+        out_copy.start()
 
     second = [py, px]
     here = [y, x]
@@ -222,18 +218,23 @@
         w = width(l, path)
         for o in range(1, 8):
             c1[l, path, o].wait_recv()
+        if l == TOP:
+            for s in range(8):
+                mask_ref[path, s] = r1[l][path][s, SL:SL + 16, 0:128].astype(F32)[0:8]
 
         def step(i, _):
             rows = pl.ds(pl.multiple_of(i * 16, 16), 16)
-            raw = [r1[l][path][s, rows, :].astype(F32) for s in range(8)]
-            for r in range(4):
-                tot = raw[0] * mask_ref[path, 0, r:r + 1, 0:w]
-                for s in range(1, 8):
-                    tot = tot + raw[s] * mask_ref[path, s, r:r + 1, 0:w]
-                if path == 1:
-                    s2[l][path][r, rows, :] = tot.astype(BF16)
-                else:
-                    tmp_ref[r, rows, 0:w] = tot
+            for lane in range(0, w, 128):
+                at = slice(lane, lane + 128)
+                raw = [r1[l][path][s, rows, at].astype(F32) for s in range(8)]
+                for r in range(4):
+                    tot = raw[0] * mask_ref[path, 0, r:r + 1, :]
+                    for s in range(1, 8):
+                        tot = tot + raw[s] * mask_ref[path, s, r:r + 1, :]
+                    if path == 1:
+                        s2[l][path][r, rows, at] = tot.astype(BF16)
+                    else:
+                        tmp_ref[r, rows, at] = tot
             return 0
 
         lax.fori_loop(0, SL // 16, step, 0)
@@ -247,57 +248,75 @@
                 s2_s.at[l, path, o], s2_r.at[l, path, o], second[path](o))
         r2[l][path][here[path]] = s2[l][path][here[path]]
 
-    def stage2(l, path):
-        w = width(l, path)
-        for o in range(1, 4):
-            c2[l, path, o].wait_recv()
-        tot = r2[l][path][0].astype(F32)
-        for s in range(1, 4):
-            tot = tot + r2[l][path][s].astype(F32)
-        tot = jnp.concatenate([tot, jnp.zeros((16, w), F32)], axis=0)
+    def stage2(l):
+        tiles = [None] * 3
+        for path in (1, 0):
+            lo, hi = cols(l, path)
+            for o in range(1, 4):
+                c2[l, path, o].wait_recv()
+            tot = r2[l][path][0].astype(F32)
+            for s in range(1, 4):
+                tot = tot + r2[l][path][s].astype(F32)
+            for lane in range(lo, hi, 128):
+                tiles[lane // 128] = tot[:, lane - lo:lane - lo + 128]
+        fill = jnp.zeros((10, 128), F32)
         for zz in range(8):
-            s3[l][path][zz] = tot[UNIT * zz:UNIT * zz + 32].astype(BF16)
+            parts = [t[UNIT * zz:UNIT * zz + UNIT] for t in tiles]
+            s3[l][zz] = jnp.concatenate(parts + [fill], axis=0).astype(BF16)
         for o in range(1, 8):
-            c3[l, path, o] = remote(
-                s3[l][path].at[(z + o) % 8], r3[l][path].at[z],
-                s3_s.at[l, path, o], s3_r.at[l, path, o], pz(o))
-        r3[l][path][z] = s3[l][path][z]
+            c3[l, o] = remote(
+                s3[l].at[(z + o) % 8], r3[l].at[z], s3_s.at[l, o], s3_r.at[l, o], pz(o))
+        r3[l][z] = s3[l][z]
 
     finals = []
 
-    def stage3(l, path):
-        lo, hi = cols(l, path)
+    def stage3(l):
         for o in range(1, 8):
-            c3[l, path, o].wait_recv()
-        tot = r3[l][path][0].astype(F32)
+            c3[l, o].wait_recv()
+        tot = r3[l][0].astype(F32)
         for s in range(1, 8):
-            tot = tot + r3[l][path][s].astype(F32)
-        fs[l][path][...] = tot[0:24]
-        xx, tt, i = final_target(l, path)
-        own = jnp.logical_and(xx == x, tt == pos)
-        dst = fin_ref.at[i, :, lo:hi]
-        far = pltpu.make_async_remote_copy(
-            src_ref=fs[l][path], dst_ref=dst, send_sem=fn_s.at[l, path], recv_sem=fn_r.at[i],
-            device_id=dev(xx, tt), device_id_type=MESH)
-        near = pltpu.make_async_copy(fs[l][path], dst, fn_r.at[i])
-
-        @pl.when(own)
-        def _():
-            near.start()
-
-        @pl.when(jnp.logical_not(own))
-        def _():
-            far.start()
-        finals.append((own, far))
-
-    for l in range(LAYERS - 1, -1, -1):
-        for stage in (stage1, stage2, stage3):
-            for path in (1, 0):
-                stage(l, path)
+            tot = tot + r3[l][s].astype(F32)
+        for ct in range(3):
+            fs[l][ct] = tot[UNIT * ct:UNIT * ct + 24]
+        for path in (1, 0):
+            lo, hi = cols(l, path)
+            tiles = pl.ds(lo // 128, (hi - lo) // 128)
+            xx, tt, i = final_target(l, path)
+            own = jnp.logical_and(xx == x, tt == pos)
+            src, dst = fs[l].at[tiles], fin_ref.at[i, tiles]
+            far = pltpu.make_async_remote_copy(
+                src_ref=src, dst_ref=dst, send_sem=fn_s.at[l, path], recv_sem=fn_r.at[i],
+                device_id=dev(xx, tt), device_id_type=MESH)
+            near = pltpu.make_async_copy(src, dst, fn_r.at[i])
+
+            @pl.when(own)
+            def _():
+                near.start()
+
+            @pl.when(jnp.logical_not(own))
+            def _():
+                far.start()
+            finals.append((own, far))
+
+    stage1(2, 1)
+    stage1(2, 0)
+    stage1(1, 1)
+    stage1(1, 0)
+    stage2(2)
+    latent_out()
+    stage1(0, 1)
+    stage1(0, 0)
+    stage2(1)
+    stage3(2)
+    stage2(0)
+    stage3(1)
+    stage3(0)
 
     for i in range(3):
         pltpu.make_async_copy(fin_ref.at[i], fin_ref.at[i], fn_r.at[i]).wait()
-    wg_ref[0] = jnp.concatenate([fin_ref[i, 0:UNIT] for i in range(3)], axis=0)
+    for ct in range(3):
+        part = jnp.concatenate([fin_ref[i, ct, 0:UNIT] for i in range(3)], axis=0)
+        wg_ref[:, 0, 128 * ct:128 * ct + 128] = part
 
     for cp in started:
         cp.wait_send()
@@ -327,38 +346,34 @@
         vmem((LAYERS, 192, CH), BF16),
         vmem((FRAMES, SPOTS, CH), BF16),
     ]
-    scratch += per(lambda w: (8, SL, w), BF16)
-    scratch += per(lambda w: (8, SL, w), BF16)
+    slices = [vmem((8, SL + 16 * (l == TOP), width(l, path)), BF16) for l in range(LAYERS) for path in range(2)]
+    scratch += slices + slices
     scratch += per(lambda w: (4, SL, w), BF16)
     scratch += per(lambda w: (4, SL, w), BF16)
-    scratch += per(lambda w: (8, 32, w), BF16)
-    scratch += per(lambda w: (8, 32, w), BF16)
-    scratch += per(lambda w: (24, w), F32)
-    scratch += [
-        vmem((4, SL, 256), F32),
-        vmem((8, 256), F32),
-        vmem((2, 8, 8, 256), F32),
-        vmem((3, 24, CH), F32),
-    ]
+    scratch += [vmem((8, 64, 128), BF16)] * LAYERS
+    scratch += [vmem((8, 64, 128), BF16)] * LAYERS
+    scratch += [vmem((3, 24, 128), F32)] * LAYERS
+    scratch += [vmem((4, SL, 256), F32), vmem((2, 8, 8, 128), F32), vmem((3, 3, 24, 128), F32)]
     dma = pltpu.SemaphoreType.DMA
-    scratch += [dma((8,)), dma((3,)), dma((3,)), dma((2, 8)), dma((2, 8))]
-    scratch += [dma((3, 2, 8)), dma((3, 2, 8)), dma((3, 2, 4)), dma((3, 2, 4)), dma((3, 2, 8)), dma((3, 2, 8))]
+    scratch += [dma((8,)), dma((3,)), dma((3,))]
+    scratch += [dma((3, 2, 8)), dma((3, 2, 8)), dma((3, 2, 4)), dma((3, 2, 4)), dma((3, 8)), dma((3, 8))]
     scratch += [dma((3, 2)), dma((3,)), dma(())]
     hbm = pl.BlockSpec(memory_space=pl.ANY)
     near = pl.BlockSpec(memory_space=pltpu.VMEM)
-    return pl.pallas_call(
+    latent_grad, block = pl.pallas_call(
         kernel,
         out_shape=(
             jax.ShapeDtypeStruct((1, FRAMES, SPOTS, CH), BF16),
-            jax.ShapeDtypeStruct((1, 3 * UNIT, CH), F32),
+            jax.ShapeDtypeStruct((3 * UNIT, 1, CH), F32),
         ),
         in_specs=[hbm, hbm, hbm, hbm, near, near, near],
         out_specs=(hbm, near),
         scratch_shapes=scratch,
         compiler_params=pltpu.CompilerParams(
-            collective_id=0, has_side_effects=True, vmem_limit_bytes=48 * 1024 * 1024),
+            collective_id=0, has_side_effects=True, vmem_limit_bytes=63 * 1024 * 1024),
         cost_estimate=pl.CostEstimate(flops=3_060_000_000, bytes_accessed=5_000_000, transcendentals=450_000),
     )(latents, caches, reward_grad, weights, biases, selected, destination)
+    return latent_grad, jnp.transpose(block, (1, 0, 2))
 
 
 def solution(mesh):

time: 82.3 us -> 63.2 us (0.77)
  Pallas kernels: 73.2 us -> 58.5 us
  local copies, waits for them, and re-layouts: 7.46 us -> 3.27 us
    pallas_call x1, Pallas kernels: 73.2 us -> 58.5 us  [body(): pl.pallas_call(kernel, out_shape=(jax.ShapeDtypeStruct((1, FRAMES, SPOTS,...]
    unnamed x13 -> x2, local copies, waits for them, and re-layouts: 6.74 us -> 3.27 us
where the time goes in v2:
time: 63.2 us; the launch traced here: 63 us
  Pallas kernels  58.5 us (93%)
  local copies, waits for them, and re-layouts  3.27 us (5%)
  between operations  1.29 us (2%)
    pallas_call x1, Pallas kernels, body(): pl.pallas_call(kernel, out_shape=(jax.ShapeDtypeStruct((1, FRAMES, SPOTS,...  58.5 us
    unnamed x2, local copies, waits for them, and re-layouts  3.27 us

profile of v2, /device:TPU:5, one launch (start us, length us, event | category | flops | bytes accessed | tf_op | source)
XLA Modules:
  0.0 63.0 jit_solution(14983654775991553996)
XLA Ops:
  1.3 58.5 %shard_map.86 = (bf16[1,4,96,384]{3,2,1,0:T(8,128)(2,1)}, f32[54,1,384]{2,1,0:T(1,128)}) custom-call(bf16[1,4,96,384]{3,2,1,0:T(8,128)(2,1)} %refs_0_.1, bf16[1,1,3,2,96,384]{5,4,3,2,1,0:T(8,128)(2,1)} %refs_1_.1, bf16[1,4,96,384]{3,2,1,0:T(8,128)(2,1)} %refs_2_.1, bf16[3,3,384,384]{3,2,1,0:T(8,128)(2,1)} %refs_3_.1, f32[3,384]{1,0:T(4,128)} %refs_4_.1, ...), custom_call_target="tpu_custom_call" | custom-call | flops 3060000000 | bytes 5000000 | tf_op jit(solution)/shard_map/pallas_call | solution.py:363
  59.8 1.7 %copy.12 = bf16[1,4,96,384]{3,2,1,0:T(8,128)(2,1)} copy(bf16[1,4,96,384]{3,2,1,0:T(8,128)(2,1)} %get-tuple-element.8) | data formatting | bytes 589824
  61.5 1.6 %copy.13 = f32[1,54,384]{2,0,1:T(1,128)} copy(f32[1,54,384]{2,0,1:T(1,128)} %bitcast.1) | data formatting | bytes 165888

commit v3 on v2

--- a/solution.py
+++ b/solution.py
@@ -45,8 +45,8 @@
 def kernel(*refs):
     it = iter(refs)
     take = lambda n: [next(it) for _ in range(n)]
-    lat_hbm, cache_hbm, rg_hbm, w_hbm, bias_ref, sel_ref, dest_ref = take(7)
-    latout_hbm, wg_ref = take(2)
+    lat_hbm, cache_hbm, rg_hbm, w_hbm, bias_hbm, sel_hbm, dest_hbm = take(7)
+    latout_hbm, fin_ref = take(2)
     w_ref, e_ref, rg_ref, sp_ref, g_ref, dpad_ref, leave_ref, in_ref, latg_ref = take(9)
     gbuf = [take(2) for _ in range(LAYERS)]
     r1 = [take(2) for _ in range(LAYERS)]
@@ -55,7 +55,7 @@
     s3 = take(LAYERS)
     r3 = take(LAYERS)
     fs = take(LAYERS)
-    (tmp_ref, mask_ref, fin_ref) = take(3)
+    (tmp_ref, mask_ref, bias_ref, sel_ref, dest_ref) = take(5)
     (ld_sem, ch_s, ch_r, s1_s, s1_r, s2_s, s2_r, s3_s, s3_r, fn_s, fn_r, out_sem) = take(12)
 
     x = lax.axis_index("clip")
@@ -68,6 +68,9 @@
     def load(name, src, dst, k):
         loads[name] = pltpu.make_async_copy(src, dst, ld_sem.at[k])
         loads[name].start()
+    load("sel", sel_hbm, sel_ref, 8)
+    load("dest", dest_hbm, dest_ref, 9)
+    load("bias", bias_hbm, bias_ref, 10)
     load("lat", lat_hbm.at[0], e_ref.at[0, pl.ds(2, 4)], 0)
     for l in range(LAYERS):
         load(("c", l), cache_hbm.at[0, 0, l], e_ref.at[l, pl.ds(0, 2)], 1 + l)
@@ -119,6 +122,8 @@
     for who in greet:
         pl.semaphore_signal(barrier, inc=1, device_id=who, device_id_type=MESH)
 
+    for name in ("sel", "dest", "bias"):
+        loads[name].wait()
     flag = jnp.max((sel_ref[...] == pos).astype(F32), axis=1, keepdims=True)
     for path in range(2):
         w = width(TOP, path)
@@ -161,6 +166,14 @@
     first = [a1, b1]
     c1 = {}
     chain = {}
+    def send1(l, path):
+        for o in range(1, 8):
+            s = (mine[path] + o) % 8
+            c1[l, path, o] = remote(
+                gbuf[l][path].at[s], r1[l][path].at[mine[path]],
+                s1_s.at[l, path, o], s1_r.at[l, path, o], first[path](o))
+        r1[l][path][mine[path]] = gbuf[l][path][mine[path]]
+
     for l in range(LAYERS - 1, -1, -1):
         if l < LAYERS - 1:
             @pl.when(pos < 63)
@@ -189,12 +202,11 @@
             lo, hi = cols(l, path)
             grads = jnp.dot(et, dp[:, lo:hi], preferred_element_type=F32)
             gbuf[l][path][:, 0:SL] = grads.astype(BF16).reshape(8, SL, hi - lo)
-            for o in range(1, 8):
-                s = (mine[path] + o) % 8
-                c1[l, path, o] = remote(
-                    gbuf[l][path].at[s], r1[l][path].at[mine[path]],
-                    s1_s.at[l, path, o], s1_r.at[l, path, o], first[path](o))
-            r1[l][path][mine[path]] = gbuf[l][path][mine[path]]
+            if l != 1:
+                send1(l, path)
+        if l == 0:
+            send1(1, 1)
+            send1(1, 0)
 
         lhs = jnp.concatenate([dpad_ref[4 - k:8 - k].reshape(ROWS, CH) for k in range(TAPS)], axis=1)
         rhs = jnp.concatenate([w_ref[l, k] for k in range(TAPS)], axis=1)
@@ -300,24 +312,20 @@
 
     stage1(2, 1)
     stage1(2, 0)
-    stage1(1, 1)
-    stage1(1, 0)
-    stage2(2)
     latent_out()
     stage1(0, 1)
     stage1(0, 0)
+    stage2(2)
+    stage1(1, 1)
+    stage1(1, 0)
+    stage2(0)
+    stage3(2)
     stage2(1)
-    stage3(2)
-    stage2(0)
+    stage3(0)
     stage3(1)
-    stage3(0)
 
     for i in range(3):
         pltpu.make_async_copy(fin_ref.at[i], fin_ref.at[i], fn_r.at[i]).wait()
-    for ct in range(3):
-        part = jnp.concatenate([fin_ref[i, ct, 0:UNIT] for i in range(3)], axis=0)
-        wg_ref[:, 0, 128 * ct:128 * ct + 128] = part
-
     for cp in started:
         cp.wait_send()
     for own, far in finals:
@@ -330,6 +338,13 @@
         for l in range(LAYERS):
             chain[l].wait_send()
     out_copy.wait()
+
+
+def finish(lat_ref, unit_ref, latout_ref, wg_ref):
+    latout_ref[...] = lat_ref[...]
+    for ct in range(3):
+        part = jnp.concatenate([unit_ref[i, ct, 0:UNIT] for i in range(3)], axis=0)
+        wg_ref[:, 0, 128 * ct:128 * ct + 128] = part
 
 
 def body(latents, caches, reward_grad, weights, biases, selected, destination):
@@ -353,26 +368,36 @@
     scratch += [vmem((8, 64, 128), BF16)] * LAYERS
     scratch += [vmem((8, 64, 128), BF16)] * LAYERS
     scratch += [vmem((3, 24, 128), F32)] * LAYERS
-    scratch += [vmem((4, SL, 256), F32), vmem((2, 8, 8, 128), F32), vmem((3, 3, 24, 128), F32)]
+    scratch += [vmem((4, SL, 256), F32), vmem((2, 8, 8, 128), F32)]
+    scratch += [vmem((LAYERS, CH), F32), vmem((1, 32), jnp.int32), vmem((1, 1), jnp.int32)]
     dma = pltpu.SemaphoreType.DMA
-    scratch += [dma((8,)), dma((3,)), dma((3,))]
+    scratch += [dma((11,)), dma((3,)), dma((3,))]
     scratch += [dma((3, 2, 8)), dma((3, 2, 8)), dma((3, 2, 4)), dma((3, 2, 4)), dma((3, 8)), dma((3, 8))]
     scratch += [dma((3, 2)), dma((3,)), dma(())]
     hbm = pl.BlockSpec(memory_space=pl.ANY)
     near = pl.BlockSpec(memory_space=pltpu.VMEM)
-    latent_grad, block = pl.pallas_call(
+    latent_grad, units = pl.pallas_call(
         kernel,
         out_shape=(
             jax.ShapeDtypeStruct((1, FRAMES, SPOTS, CH), BF16),
-            jax.ShapeDtypeStruct((3 * UNIT, 1, CH), F32),
+            jax.ShapeDtypeStruct((3, 3, 24, 128), F32),
         ),
-        in_specs=[hbm, hbm, hbm, hbm, near, near, near],
-        out_specs=(hbm, near),
+        in_specs=[hbm] * 7,
+        out_specs=(hbm, hbm),
         scratch_shapes=scratch,
         compiler_params=pltpu.CompilerParams(
             collective_id=0, has_side_effects=True, vmem_limit_bytes=63 * 1024 * 1024),
         cost_estimate=pl.CostEstimate(flops=3_060_000_000, bytes_accessed=5_000_000, transcendentals=450_000),
     )(latents, caches, reward_grad, weights, biases, selected, destination)
+    latent_grad, block = pl.pallas_call(
+        finish,
+        out_shape=(
+            jax.ShapeDtypeStruct((1, FRAMES, SPOTS, CH), BF16),
+            jax.ShapeDtypeStruct((3 * UNIT, 1, CH), F32),
+        ),
+        in_specs=[near, near],
+        out_specs=(near, near),
+    )(latent_grad, units)
     return latent_grad, jnp.transpose(block, (1, 0, 2))
 
 

time: 63.2 us -> 58 us (0.918)
  the two profiles are of different devices: /device:TPU:5 before, /device:TPU:17 now
where the time goes in v3:
time: 58 us; the launch traced here: 57.8 us
  Pallas kernels  56.5 us (97%)
  between operations  1.29 us (2%)
    pallas_call x1, Pallas kernels, body(): pl.pallas_call(kernel, out_shape=(jax.ShapeDtypeStruct((1, FRAMES, SPOTS,...  54.8 us
    pallas_call x1, Pallas kernels, body(): pl.pallas_call(finish, out_shape=(jax.ShapeDtypeStruct((1, FRAMES, SPOTS,...  1.75 us

profile of v3, /device:TPU:17, one launch (start us, length us, event | category | flops | bytes accessed | tf_op | source)
XLA Modules:
  0.0 57.8 jit_solution(4074579047230653216)
XLA Ops:
  1.3 54.8 %shard_map.86 = (bf16[1,4,96,384]{3,2,1,0:T(8,128)(2,1)}, f32[3,3,24,128]{3,2,1,0:T(8,128)}) custom-call(bf16[1,4,96,384]{3,2,1,0:T(8,128)(2,1)} %refs_0_.1, bf16[1,1,3,2,96,384]{5,4,3,2,1,0:T(8,128)(2,1)} %refs_1_.1, bf16[1,4,96,384]{3,2,1,0:T(8,128)(2,1)} %refs_2_.1, bf16[3,3,384,384]{3,2,1,0:T(8,128)(2,1)} %refs_3_.1, f32[3,384]{1,0:T(4,128)} %refs_4_.1, ...), custom_call_target="tpu_custom_call" | custom-call | flops 3060000000 | bytes 5000000 | tf_op jit(solution)/shard_map/pallas_call | solution.py:379
  56.1 1.7 %shard_map.87 = (bf16[1,4,96,384]{3,2,1,0:T(8,128)(2,1)}, f32[54,1,384]{2,1,0:T(1,128)}) custom-call(bf16[1,4,96,384]{3,2,1,0:T(8,128)(2,1)} %get-tuple-element.6.lat_ref, f32[3,3,24,128]{3,2,1,0:T(8,128)} %get-tuple-element.7.unit_ref), custom_call_target="tpu_custom_call" | custom-call | tf_op jit(solution)/shard_map/pallas_call | solution.py:392

commit v4 on v3

--- a/solution.py
+++ b/solution.py
@@ -35,11 +35,6 @@
 
 def task_of(y, z, c):
     return y * 16 + z * 2 + c
-
-
-def unit_target(layer, unit):
-    u = layer * 64 + unit
-    return u // 3, u % 3
 
 
 def kernel(*refs):
@@ -55,7 +50,7 @@
     s3 = take(LAYERS)
     r3 = take(LAYERS)
     fs = take(LAYERS)
-    (tmp_ref, mask_ref, bias_ref, sel_ref, dest_ref) = take(5)
+    (mask_ref, bias_ref, sel_ref, dest_ref) = take(4)
     (ld_sem, ch_s, ch_r, s1_s, s1_r, s2_s, s2_r, s3_s, s3_r, fn_s, fn_r, out_sem) = take(12)
 
     x = lax.axis_index("clip")
@@ -97,28 +92,29 @@
     def pz(o):
         return dev(x, task_of(y, (z + o) % 8, c))
 
-    unit_b = 8 * (2 * y + c) + z
-    unit_a = 8 * (2 * x + c) + 2 * y + z % 2
-
-    def final_target(l, path):
+    place1 = [2 * x + c, 2 * y + c]
+    replica = [y, x]
+
+    def z_shift(l):
+        return 2 + 2 * l + l // 2
+
+    def owner(l, path):
+        u = 64 * l + 8 * ((z - z_shift(l) + 8) % 8) + place1[path]
+        return replica[path], u // 3, u % 3
+
+    def source(i, path):
+        u = 3 * pos + i
+        l, m, s = u // 64, (u % 64) // 8, u % 8
+        zz = (m + z_shift(l)) % 8
         if path == 1:
-            t, i = unit_target(l, unit_b)
-            return x, t, i
-        t, i = unit_target(l, unit_a)
-        return z // 2, t, i
-
-    def final_source(i, path):
-        u = 3 * pos + i
-        j = u % 64
-        if path == 1:
-            return x, task_of(j // 16, j % 8, (j // 8) % 2)
-        return j // 16, task_of((j % 8) // 2, 2 * x + j % 2, (j // 8) % 2)
+            return dev(x, task_of(s // 2, zz, s % 2))
+        return dev(s // 2, task_of(x, zz, s % 2))
 
     barrier = pltpu.get_barrier_semaphore()
     greet = [b1(o) for o in range(1, 8)] + [a1(o) for o in range(1, 8)]
     greet += [px(o) for o in range(1, 4)] + [py(o) for o in range(1, 4)] + [pz(o) for o in range(1, 8)]
     greet += [dev(x, (pos + 1) % 64)]
-    greet += [dev(*final_source(i, path)) for i in range(3) for path in range(2)]
+    greet += [source(i, path) for i in range(3) for path in range(2)]
     for who in greet:
         pl.semaphore_signal(barrier, inc=1, device_id=who, device_id_type=MESH)
 
@@ -162,7 +158,7 @@
     loads["rg"].wait()
     g_ref[...] = rg_ref[...].reshape(ROWS, CH).astype(F32) * flag
 
-    mine = [2 * x + c, 2 * y + c]
+    mine = place1
     first = [a1, b1]
     c1 = {}
     chain = {}
@@ -182,28 +178,38 @@
             g_ref[pl.ds(192, 192)] += in_ref[l + 1].astype(F32)
         d = (g_ref[...] * sp_ref[l]).astype(BF16)
         dpad_ref[pl.ds(2, 4)] = d.reshape(FRAMES, SPOTS, CH)
-        lhs = jnp.concatenate([dpad_ref[2:4].reshape(192, CH), dpad_ref[1:3].reshape(192, CH)], axis=1)
-        rhs = jnp.concatenate([w_ref[l, 0], w_ref[l, 1]], axis=1)
-        lead = lax.dot_general(lhs, rhs, (((1,), (1,)), ((), ())), preferred_element_type=F32)
-        leave_ref[l] = lead.astype(BF16)
-        chain[l] = pltpu.make_async_remote_copy(
-            src_ref=leave_ref.at[l], dst_ref=in_ref.at[l], send_sem=ch_s.at[l], recv_sem=ch_r.at[l],
-            device_id=dev(x, (pos + 63) % 64), device_id_type=MESH)
-
-        @pl.when(pos > 0)
-        def _(l=l):
-            chain[l].start()
-
-        pad = jnp.zeros((32, CH), BF16)
-        et = jnp.concatenate([v for f in range(6) for v in (e_ref[l, f], pad)], axis=0).T
-        et = jnp.concatenate([et[:, 128 * k:128 * k + 512] for k in range(TAPS)], axis=0)
-        dp = jnp.concatenate([v for f in range(FRAMES) for v in (dpad_ref[2 + f], pad)], axis=0)
-        for path in (1, 0):
-            lo, hi = cols(l, path)
-            grads = jnp.dot(et, dp[:, lo:hi], preferred_element_type=F32)
-            gbuf[l][path][:, 0:SL] = grads.astype(BF16).reshape(8, SL, hi - lo)
-            if l != 1:
-                send1(l, path)
+        def lead_out(l=l, d=d):
+            lhs = jnp.concatenate([dpad_ref[2:4].reshape(192, CH), dpad_ref[1:3].reshape(192, CH)], axis=1)
+            rhs = jnp.concatenate([w_ref[l, 0], w_ref[l, 1]], axis=1)
+            lead = lax.dot_general(lhs, rhs, (((1,), (1,)), ((), ())), preferred_element_type=F32)
+            leave_ref[l] = lead.astype(BF16)
+            chain[l] = pltpu.make_async_remote_copy(
+                src_ref=leave_ref.at[l], dst_ref=in_ref.at[l], send_sem=ch_s.at[l], recv_sem=ch_r.at[l],
+                device_id=dev(x, (pos + 63) % 64), device_id_type=MESH)
+
+            @pl.when(pos > 0)
+            def _(l=l):
+                chain[l].start()
+
+        def kernel_grad(l=l):
+            pad = jnp.zeros((32, CH), BF16)
+            et = jnp.concatenate([v for f in range(6) for v in (e_ref[l, f], pad)], axis=0).T
+            et = jnp.concatenate([et[:, 128 * k:128 * k + 512] for k in range(TAPS)], axis=0)
+            dp = jnp.concatenate([v for f in range(FRAMES) for v in (dpad_ref[2 + f], pad)], axis=0)
+            for path in (1, 0):
+                lo, hi = cols(l, path)
+                grads = jnp.dot(et, dp[:, lo:hi], preferred_element_type=F32)
+                for s in range(8):
+                    rows = [grads[SL * m + UNIT * s:SL * m + UNIT * s + UNIT] for m in range(8)]
+                    gbuf[l][path][s, 0:SL] = jnp.concatenate(rows, axis=0).astype(BF16)
+                if l != 1:
+                    send1(l, path)
+        if l == LAYERS - 1:
+            kernel_grad()
+            lead_out()
+        else:
+            lead_out()
+            kernel_grad()
         if l == 0:
             send1(1, 1)
             send1(1, 0)
@@ -243,17 +249,10 @@
                     tot = raw[0] * mask_ref[path, 0, r:r + 1, :]
                     for s in range(1, 8):
                         tot = tot + raw[s] * mask_ref[path, s, r:r + 1, :]
-                    if path == 1:
-                        s2[l][path][r, rows, at] = tot.astype(BF16)
-                    else:
-                        tmp_ref[r, rows, at] = tot
+                    s2[l][path][r, rows, at] = tot.astype(BF16)
             return 0
 
         lax.fori_loop(0, SL // 16, step, 0)
-        if path == 0:
-            for yy in range(4):
-                s2[l][path][yy] = jnp.concatenate(
-                    [tmp_ref[r, 36 * yy:36 * yy + 36, 0:w] for r in range(4)], axis=0).astype(BF16)
         for o in range(1, 4):
             c2[l, path, o] = remote(
                 s2[l][path].at[(here[path] + o) % 4], r2[l][path].at[here[path]],
@@ -272,13 +271,14 @@
             for lane in range(lo, hi, 128):
                 tiles[lane // 128] = tot[:, lane - lo:lane - lo + 128]
         fill = jnp.zeros((10, 128), F32)
-        for zz in range(8):
-            parts = [t[UNIT * zz:UNIT * zz + UNIT] for t in tiles]
-            s3[l][zz] = jnp.concatenate(parts + [fill], axis=0).astype(BF16)
+        for m in range(8):
+            parts = [t[UNIT * m:UNIT * m + UNIT] for t in tiles]
+            s3[l][m] = jnp.concatenate(parts + [fill], axis=0).astype(BF16)
+        mine3 = (z - z_shift(l) + 8) % 8
         for o in range(1, 8):
             c3[l, o] = remote(
-                s3[l].at[(z + o) % 8], r3[l].at[z], s3_s.at[l, o], s3_r.at[l, o], pz(o))
-        r3[l][z] = s3[l][z]
+                s3[l].at[(mine3 + o) % 8], r3[l].at[z], s3_s.at[l, o], s3_r.at[l, o], pz(o))
+        r3[l][z] = s3[l][mine3]
 
     finals = []
 
@@ -288,12 +288,13 @@
         tot = r3[l][0].astype(F32)
         for s in range(1, 8):
             tot = tot + r3[l][s].astype(F32)
+        tot = jnp.concatenate([tot, jnp.zeros((8, 128), F32)], axis=0)
         for ct in range(3):
-            fs[l][ct] = tot[UNIT * ct:UNIT * ct + 24]
+            fs[l][ct] = tot[UNIT * ct:UNIT * ct + 32].astype(BF16)
         for path in (1, 0):
             lo, hi = cols(l, path)
             tiles = pl.ds(lo // 128, (hi - lo) // 128)
-            xx, tt, i = final_target(l, path)
+            xx, tt, i = owner(l, path)
             own = jnp.logical_and(xx == x, tt == pos)
             src, dst = fs[l].at[tiles], fin_ref.at[i, tiles]
             far = pltpu.make_async_remote_copy(
@@ -302,17 +303,16 @@
             near = pltpu.make_async_copy(src, dst, fn_r.at[i])
 
             @pl.when(own)
-            def _():
+            def _(near=near):
                 near.start()
 
             @pl.when(jnp.logical_not(own))
-            def _():
+            def _(far=far):
                 far.start()
             finals.append((own, far))
 
     stage1(2, 1)
     stage1(2, 0)
-    latent_out()
     stage1(0, 1)
     stage1(0, 0)
     stage2(2)
@@ -321,11 +321,13 @@
     stage2(0)
     stage3(2)
     stage2(1)
+    latent_out()
     stage3(0)
     stage3(1)
 
     for i in range(3):
         pltpu.make_async_copy(fin_ref.at[i], fin_ref.at[i], fn_r.at[i]).wait()
+
     for cp in started:
         cp.wait_send()
     for own, far in finals:
@@ -343,7 +345,7 @@
 def finish(lat_ref, unit_ref, latout_ref, wg_ref):
     latout_ref[...] = lat_ref[...]
     for ct in range(3):
-        part = jnp.concatenate([unit_ref[i, ct, 0:UNIT] for i in range(3)], axis=0)
+        part = jnp.concatenate([unit_ref[i, ct].astype(F32)[0:UNIT] for i in range(3)], axis=0)
         wg_ref[:, 0, 128 * ct:128 * ct + 128] = part
 
 
@@ -365,10 +367,9 @@
     scratch += slices + slices
     scratch += per(lambda w: (4, SL, w), BF16)
     scratch += per(lambda w: (4, SL, w), BF16)
-    scratch += [vmem((8, 64, 128), BF16)] * LAYERS
-    scratch += [vmem((8, 64, 128), BF16)] * LAYERS
-    scratch += [vmem((3, 24, 128), F32)] * LAYERS
-    scratch += [vmem((4, SL, 256), F32), vmem((2, 8, 8, 128), F32)]
+    scratch += [vmem((8, 64, 128), BF16)] * (2 * LAYERS)
+    scratch += [vmem((3, 32, 128), BF16)] * LAYERS
+    scratch += [vmem((2, 8, 8, 128), F32)]
     scratch += [vmem((LAYERS, CH), F32), vmem((1, 32), jnp.int32), vmem((1, 1), jnp.int32)]
     dma = pltpu.SemaphoreType.DMA
     scratch += [dma((11,)), dma((3,)), dma((3,))]
@@ -380,7 +381,7 @@
         kernel,
         out_shape=(
             jax.ShapeDtypeStruct((1, FRAMES, SPOTS, CH), BF16),
-            jax.ShapeDtypeStruct((3, 3, 24, 128), F32),
+            jax.ShapeDtypeStruct((3, 3, 32, 128), BF16),
         ),
         in_specs=[hbm] * 7,
         out_specs=(hbm, hbm),

time: 58 us -> 55 us (0.948)
  Pallas kernels: 56.5 us -> 53.6 us
    pallas_call x1, Pallas kernels: 54.8 us -> 51.9 us  [body(): pl.pallas_call(kernel, out_shape=(jax.ShapeDtypeStruct((1, FRAMES, SPOTS,...]
where the time goes in v4:
time: 55 us; the launch traced here: 54.9 us
  Pallas kernels  53.6 us (97%)
  between operations  1.29 us (2%)
    pallas_call x1, Pallas kernels, body(): pl.pallas_call(kernel, out_shape=(jax.ShapeDtypeStruct((1, FRAMES, SPOTS,...  51.9 us
    pallas_call x1, Pallas kernels, body(): pl.pallas_call(finish, out_shape=(jax.ShapeDtypeStruct((1, FRAMES, SPOTS,...  1.73 us

profile of v4, /device:TPU:17, one launch (start us, length us, event | category | flops | bytes accessed | tf_op | source)
XLA Modules:
  0.0 54.9 jit_solution(2558802743852479063)
XLA Ops:
  1.3 51.9 %shard_map.86 = (bf16[1,4,96,384]{3,2,1,0:T(8,128)(2,1)}, bf16[3,3,32,128]{3,2,1,0:T(8,128)(2,1)}) custom-call(bf16[1,4,96,384]{3,2,1,0:T(8,128)(2,1)} %refs_0_.1, bf16[1,1,3,2,96,384]{5,4,3,2,1,0:T(8,128)(2,1)} %refs_1_.1, bf16[1,4,96,384]{3,2,1,0:T(8,128)(2,1)} %refs_2_.1, bf16[3,3,384,384]{3,2,1,0:T(8,128)(2,1)} %refs_3_.1, f32[3,384]{1,0:T(4,128)} %refs_4_.1, ...), custom_call_target="tpu_custom_call" | custom-call | flops 3060000000 | bytes 5000000 | tf_op jit(solution)/shard_map/pallas_call | solution.py:380
  53.2 1.7 %shard_map.87 = (bf16[1,4,96,384]{3,2,1,0:T(8,128)(2,1)}, f32[54,1,384]{2,1,0:T(1,128)}) custom-call(bf16[1,4,96,384]{3,2,1,0:T(8,128)(2,1)} %get-tuple-element.6.lat_ref, bf16[3,3,32,128]{3,2,1,0:T(8,128)(2,1)} %get-tuple-element.7.unit_ref), custom_call_target="tpu_custom_call" | custom-call | tf_op jit(solution)/shard_map/pallas_call | solution.py:393

commit v5 on v4

--- a/solution.py
+++ b/solution.py
@@ -163,7 +163,7 @@
     c1 = {}
     chain = {}
     def send1(l, path):
-        for o in range(1, 8):
+        for o in (4, 3, 5, 2, 6, 1, 7):
             s = (mine[path] + o) % 8
             c1[l, path, o] = remote(
                 gbuf[l][path].at[s], r1[l][path].at[mine[path]],
@@ -253,7 +253,7 @@
             return 0
 
         lax.fori_loop(0, SL // 16, step, 0)
-        for o in range(1, 4):
+        for o in (2, 1, 3):
             c2[l, path, o] = remote(
                 s2[l][path].at[(here[path] + o) % 4], r2[l][path].at[here[path]],
                 s2_s.at[l, path, o], s2_r.at[l, path, o], second[path](o))
@@ -275,7 +275,7 @@
             parts = [t[UNIT * m:UNIT * m + UNIT] for t in tiles]
             s3[l][m] = jnp.concatenate(parts + [fill], axis=0).astype(BF16)
         mine3 = (z - z_shift(l) + 8) % 8
-        for o in range(1, 8):
+        for o in (4, 3, 5, 2, 6, 1, 7):
             c3[l, o] = remote(
                 s3[l].at[(mine3 + o) % 8], r3[l].at[z], s3_s.at[l, o], s3_r.at[l, o], pz(o))
         r3[l][z] = s3[l][mine3]
@@ -319,11 +319,11 @@
     stage1(1, 1)
     stage1(1, 0)
     stage2(0)
+    stage2(1)
     stage3(2)
-    stage2(1)
-    latent_out()
     stage3(0)
     stage3(1)
+    latent_out()
 
     for i in range(3):
         pltpu.make_async_copy(fin_ref.at[i], fin_ref.at[i], fn_r.at[i]).wait()
@@ -342,11 +342,23 @@
     out_copy.wait()
 
 
-def finish(lat_ref, unit_ref, latout_ref, wg_ref):
-    latout_ref[...] = lat_ref[...]
+def finish(lat_ref, units_ref, latout_ref, wgout_ref, lat, unit_ref, wg_ref, sem_in, sem_out):
+    into = [pltpu.make_async_copy(units_ref, unit_ref, sem_in.at[FRAMES])]
+    into += [pltpu.make_async_copy(lat_ref.at[0, f], lat.at[f], sem_in.at[f]) for f in range(FRAMES)]
+    out = [pltpu.make_async_copy(lat.at[f], latout_ref.at[0, f], sem_out.at[f]) for f in range(FRAMES)]
+    out += [pltpu.make_async_copy(wg_ref, wgout_ref, sem_out.at[FRAMES])]
+    for copy in into:
+        copy.start()
+    into[0].wait()
     for ct in range(3):
         part = jnp.concatenate([unit_ref[i, ct].astype(F32)[0:UNIT] for i in range(3)], axis=0)
         wg_ref[:, 0, 128 * ct:128 * ct + 128] = part
+    out[FRAMES].start()
+    for f in range(FRAMES):
+        into[1 + f].wait()
+        out[f].start()
+    for copy in out:
+        copy.wait()
 
 
 def body(latents, caches, reward_grad, weights, biases, selected, destination):
@@ -376,7 +388,6 @@
     scratch += [dma((3, 2, 8)), dma((3, 2, 8)), dma((3, 2, 4)), dma((3, 2, 4)), dma((3, 8)), dma((3, 8))]
     scratch += [dma((3, 2)), dma((3,)), dma(())]
     hbm = pl.BlockSpec(memory_space=pl.ANY)
-    near = pl.BlockSpec(memory_space=pltpu.VMEM)
     latent_grad, units = pl.pallas_call(
         kernel,
         out_shape=(
@@ -396,8 +407,15 @@
             jax.ShapeDtypeStruct((1, FRAMES, SPOTS, CH), BF16),
             jax.ShapeDtypeStruct((3 * UNIT, 1, CH), F32),
         ),
-        in_specs=[near, near],
-        out_specs=(near, near),
+        in_specs=[hbm, hbm],
+        out_specs=(hbm, hbm),
+        scratch_shapes=[
+            vmem((FRAMES, SPOTS, CH), BF16),
+            vmem((3, 3, 32, 128), BF16),
+            vmem((3 * UNIT, 1, CH), F32),
+            pltpu.SemaphoreType.DMA((FRAMES + 1,)),
+            pltpu.SemaphoreType.DMA((FRAMES + 1,)),
+        ],
     )(latent_grad, units)
     return latent_grad, jnp.transpose(block, (1, 0, 2))
 

time: 55 us -> 54.8 us (level)
  no operation moved by 1% of the time
where the time goes in v5:
time: 54.8 us; the launch traced here: 54.7 us
  Pallas kernels  53.4 us (97%)
  between operations  1.29 us (2%)
    pallas_call x1, Pallas kernels, body(): pl.pallas_call(kernel, out_shape=(jax.ShapeDtypeStruct((1, FRAMES, SPOTS,...  51.7 us
    pallas_call x1, Pallas kernels, body(): pl.pallas_call(finish, out_shape=(jax.ShapeDtypeStruct((1, FRAMES, SPOTS,...  1.76 us

profile of v5, /device:TPU:17, one launch (start us, length us, event | category | flops | bytes accessed | tf_op | source)
XLA Modules:
  0.0 54.7 jit_solution(556687609896760523)
XLA Ops:
  1.3 51.7 %shard_map.86 = (bf16[1,4,96,384]{3,2,1,0:T(8,128)(2,1)}, bf16[3,3,32,128]{3,2,1,0:T(8,128)(2,1)}) custom-call(bf16[1,4,96,384]{3,2,1,0:T(8,128)(2,1)} %refs_0_.1, bf16[1,1,3,2,96,384]{5,4,3,2,1,0:T(8,128)(2,1)} %refs_1_.1, bf16[1,4,96,384]{3,2,1,0:T(8,128)(2,1)} %refs_2_.1, bf16[3,3,384,384]{3,2,1,0:T(8,128)(2,1)} %refs_3_.1, f32[3,384]{1,0:T(4,128)} %refs_4_.1, ...), custom_call_target="tpu_custom_call" | custom-call | flops 3060000000 | bytes 5000000 | tf_op jit(solution)/shard_map/pallas_call | solution.py:391
  52.9 1.8 %shard_map.87 = (bf16[1,4,96,384]{3,2,1,0:T(8,128)(2,1)}, f32[54,1,384]{2,1,0:T(1,128)}) custom-call(bf16[1,4,96,384]{3,2,1,0:T(8,128)(2,1)} %get-tuple-element.6.lat_ref, bf16[3,3,32,128]{3,2,1,0:T(8,128)(2,1)} %get-tuple-element.7.units_ref), custom_call_target="tpu_custom_call" | custom-call | tf_op jit(solution)/shard_map/pallas_call | solution.py:404
